TPU v7x, 128 devices: a whole 4x4x4 slice. The times are simulated.
128 devices in a mesh: replica: 4 (over x_hi, core), shard: 32 (over z, x_lo, y).
Axes of the slice: x: 4 (x_hi: 2, x_lo: 2; x = x_hi * 2 + x_lo), y: 4, z: 4, core: 2. Of those that a mesh axis runs over, the one named last changes fastest.
Arguments:
- tokens: bfloat16 [16384, 2048], P(('replica', 'shard')), may hold values from -6 to 6
- segment_ids: int32 [128, 128], P(('replica', 'shard')), may hold values from 0 to 3, never falling along the last dimension, each value on 1 to 64 neighbouring positions
- cotangent: bfloat16 [16384, 2048], P(('replica', 'shard')), may hold values from -6 to 6
- ln1_gain: bfloat16 [2048], P('shard'), may hold values from 0.5 to 1.5
- ln1_bias: bfloat16 [2048], P('shard'), may hold values from -2 to 2
- qkv_weight: bfloat16 [2048, 6144], P('shard'), may hold values from -0.125 to 0.125
- qkv_bias: bfloat16 [6144], P('shard'), may hold values from -3 to 3
- out_weight: bfloat16 [2048, 2048], P('shard'), may hold values from -0.375 to 0.375
- ln2_gain: bfloat16 [2048], P('shard'), may hold values from 0.5 to 1.5
- ln2_bias: bfloat16 [2048], P('shard'), may hold values from -2 to 2
- gate_weight: bfloat16 [2048, 5632], P('shard'), may hold values from -0.125 to 0.125
- up_weight: bfloat16 [2048, 5632], P('shard'), may hold values from -0.125 to 0.125
- down_weight: bfloat16 [5632, 2048], P('shard'), may hold values from -0.15625 to 0.15625
Outputs:
- activations: bfloat16 [16384, 2048], P(('replica', 'shard'))
- input_grad: bfloat16 [16384, 2048], P(('replica', 'shard'))
- ln1_gain_grad: float32 [2048], P('shard')
- ln1_bias_grad: float32 [2048], P('shard')
- qkv_weight_grad: float32 [2048, 6144], P('shard')
- qkv_bias_grad: float32 [6144], P('shard')
- out_weight_grad: float32 [2048, 2048], P('shard')
- ln2_gain_grad: float32 [2048], P('shard')
- ln2_bias_grad: float32 [2048], P('shard')
- gate_weight_grad: float32 [2048, 5632], P('shard')
- up_weight_grad: float32 [2048, 5632], P('shard')
- down_weight_grad: float32 [5632, 2048], P('shard')
Inputs may be any that keep to these rules, and one draw needn't show every extreme that they name: `segment_ids`: in each sequence the ids never fall from one position to the next; each segment holds 1 to half of 128 positions, and one holds exactly that many.
All inputs are finite; a program needn't handle non-finite values.
Results may differ from a plain program's by a relative error of at most 0.029.
Values may be sent and summed in bfloat16 or wider, within the bound.
A program may use at most 384 MiB of HBM per device.

v0:
```python
import jax
import jax.numpy as jnp
from jax import lax
from jax.sharding import PartitionSpec as P

D = 2048
HEADS = 32
HEAD_DIM = 64
ROT = 16


norm_epsilon = 1e-05
masked_score = -1000000000.0


def normalize(values):
    center = values - jnp.mean(values, axis=-1, keepdims=True)
    inverse = lax.rsqrt(jnp.mean(center * center, axis=-1, keepdims=True) + norm_epsilon)
    return (center * inverse, inverse)


def norm_back(grad_entry, normed, inverse, gain):
    scaled = grad_entry * gain
    return inverse * (
        scaled
        - jnp.mean(scaled, axis=-1, keepdims=True)
        - normed * jnp.mean(scaled * normed, axis=-1, keepdims=True)
    )


def layout(segments):
    length = segments.shape[1]
    same = segments[:, :, None] == segments[:, None, :]
    query_index = lax.broadcasted_iota(jnp.int32, (length, length), 0)
    key_index = lax.broadcasted_iota(jnp.int32, (length, length), 1)
    allowed = same & (key_index <= query_index)[None]
    places = jnp.sum((same & (key_index < query_index)[None]).astype(jnp.int32), axis=-1).astype(
        jnp.float32
    )
    half_rot = ROT // 2
    freqs = 10000.0 ** (-(jnp.arange(half_rot, dtype=jnp.float32) * 2.0) / ROT)
    angles = places[:, :, None, None] * freqs
    return (allowed[:, None], jnp.cos(angles), jnp.sin(angles))


def rotate(values, cosine, sine):
    half_rot = ROT // 2
    first = values[..., :half_rot]
    second = values[..., half_rot:ROT]
    return jnp.concatenate(
        [first * cosine - second * sine, second * cosine + first * sine, values[..., ROT:]], axis=-1
    )


def attention_probs(queries, keys, allowed, logsum):
    scores = jnp.einsum(
        "slhd,smhd->shlm", queries, keys, preferred_element_type=jnp.float32
    ) * HEAD_DIM ** (-0.5)
    scores = jnp.where(allowed, scores, masked_score)
    return jnp.exp(scores - logsum)


def local(
    tokens,
    segment_ids,
    cotangent,
    ln1_gain,
    ln1_bias,
    qkv_weight,
    qkv_bias,
    out_weight,
    ln2_gain,
    ln2_bias,
    gate_weight,
    up_weight,
    down_weight,
):
    sequences = segment_ids.shape[0]
    length = segment_ids.shape[1]
    row_count = sequences * length
    scale = HEAD_DIM ** (-0.5)
    allowed, cosine, sine = layout(segment_ids)
    gain_one, bias_one, weight_qkv, bias_qkv, weight_out = (
        lax.all_gather(ln1_gain, "shard", axis=0, tiled=True),
        lax.all_gather(ln1_bias, "shard", axis=0, tiled=True),
        lax.all_gather(qkv_weight, "shard", axis=0, tiled=True),
        lax.all_gather(qkv_bias, "shard", axis=0, tiled=True),
        lax.all_gather(out_weight, "shard", axis=0, tiled=True),
    )
    inputs = tokens.astype(jnp.float32)
    normed_one, inverse_one = normalize(inputs)
    entry_one = (normed_one * gain_one.astype(jnp.float32) + bias_one.astype(jnp.float32)).astype(
        jnp.bfloat16
    )
    projected = jnp.dot(
        entry_one, weight_qkv, preferred_element_type=jnp.float32
    ) + bias_qkv.astype(jnp.float32)
    projected = projected.reshape(sequences, length, 3, HEADS, HEAD_DIM)
    queries = rotate(projected[:, :, 0], cosine, sine).astype(jnp.bfloat16)
    keys = rotate(projected[:, :, 1], cosine, sine).astype(jnp.bfloat16)
    values = projected[:, :, 2].astype(jnp.bfloat16)
    scores = (
        jnp.einsum("slhd,smhd->shlm", queries, keys, preferred_element_type=jnp.float32) * scale
    )
    scores = jnp.where(allowed, scores, masked_score)
    peak = jnp.max(scores, axis=-1, keepdims=True)
    expos = jnp.exp(scores - peak)
    totals = jnp.sum(expos, axis=-1, keepdims=True)
    logsum = peak + jnp.log(totals)
    probs = expos / totals
    mixed = jnp.einsum(
        "shlm,smhd->slhd", probs.astype(jnp.bfloat16), values, preferred_element_type=jnp.float32
    )
    mixed = mixed.reshape(row_count, D).astype(jnp.bfloat16)
    middle = inputs + jnp.dot(mixed, weight_out, preferred_element_type=jnp.float32)
    gain_two, bias_two, weight_gate, weight_up, weight_down = (
        lax.all_gather(ln2_gain, "shard", axis=0, tiled=True),
        lax.all_gather(ln2_bias, "shard", axis=0, tiled=True),
        lax.all_gather(gate_weight, "shard", axis=0, tiled=True),
        lax.all_gather(up_weight, "shard", axis=0, tiled=True),
        lax.all_gather(down_weight, "shard", axis=0, tiled=True),
    )
    normed_two, inverse_two = normalize(middle)
    entry_two = (normed_two * gain_two.astype(jnp.float32) + bias_two.astype(jnp.float32)).astype(
        jnp.bfloat16
    )
    gate = jnp.dot(entry_two, weight_gate, preferred_element_type=jnp.float32)
    upward = jnp.dot(entry_two, weight_up, preferred_element_type=jnp.float32)
    sigmoid = jax.nn.sigmoid(gate)
    hidden = (gate * sigmoid * upward).astype(jnp.bfloat16)
    result = middle + jnp.dot(hidden, weight_down, preferred_element_type=jnp.float32)
    gain_two, bias_two, weight_gate, weight_up, weight_down = (
        lax.all_gather(ln2_gain, "shard", axis=0, tiled=True),
        lax.all_gather(ln2_bias, "shard", axis=0, tiled=True),
        lax.all_gather(gate_weight, "shard", axis=0, tiled=True),
        lax.all_gather(up_weight, "shard", axis=0, tiled=True),
        lax.all_gather(down_weight, "shard", axis=0, tiled=True),
    )
    grad_top = cotangent.astype(jnp.float32)
    down_weight_grad = jnp.einsum(
        "tf,td->fd", hidden, cotangent, preferred_element_type=jnp.float32
    )
    grad_hidden = (
        jnp.einsum("td,fd->tf", cotangent, weight_down, preferred_element_type=jnp.float32)
        .astype(jnp.bfloat16)
        .astype(jnp.float32)
    )
    grad_gate = (grad_hidden * upward * sigmoid * (1.0 + gate * (1.0 - sigmoid))).astype(
        jnp.bfloat16
    )
    grad_up = (grad_hidden * gate * sigmoid).astype(jnp.bfloat16)
    gate_weight_grad = jnp.einsum(
        "td,tf->df", entry_two, grad_gate, preferred_element_type=jnp.float32
    )
    up_weight_grad = jnp.einsum("td,tf->df", entry_two, grad_up, preferred_element_type=jnp.float32)
    grad_entry_two = jnp.einsum(
        "tf,df->td", grad_gate, weight_gate, preferred_element_type=jnp.float32
    )
    grad_entry_two = grad_entry_two + jnp.einsum(
        "tf,df->td", grad_up, weight_up, preferred_element_type=jnp.float32
    )
    ln2_gain_grad = jnp.sum(grad_entry_two * normed_two, axis=0)
    ln2_bias_grad = jnp.sum(grad_entry_two, axis=0)
    grad_middle = grad_top + norm_back(
        grad_entry_two, normed_two, inverse_two, gain_two.astype(jnp.float32)
    )
    gain_two_sum, bias_two_sum, gate_sum, up_sum, down_sum = (
        lax.psum_scatter(
            ln2_gain_grad.astype(jnp.bfloat16), "shard", scatter_dimension=0, tiled=True
        ).astype(jnp.float32),
        lax.psum_scatter(
            ln2_bias_grad.astype(jnp.bfloat16), "shard", scatter_dimension=0, tiled=True
        ).astype(jnp.float32),
        lax.psum_scatter(
            gate_weight_grad.astype(jnp.bfloat16), "shard", scatter_dimension=0, tiled=True
        ).astype(jnp.float32),
        lax.psum_scatter(
            up_weight_grad.astype(jnp.bfloat16), "shard", scatter_dimension=0, tiled=True
        ).astype(jnp.float32),
        lax.psum_scatter(
            down_weight_grad.astype(jnp.bfloat16), "shard", scatter_dimension=0, tiled=True
        ).astype(jnp.float32),
    )
    gain_two_sum, bias_two_sum, gate_sum, up_sum, down_sum = (
        lax.psum(gain_two_sum.astype(jnp.bfloat16), "replica").astype(jnp.float32),
        lax.psum(bias_two_sum.astype(jnp.bfloat16), "replica").astype(jnp.float32),
        lax.psum(gate_sum.astype(jnp.bfloat16), "replica").astype(jnp.float32),
        lax.psum(up_sum.astype(jnp.bfloat16), "replica").astype(jnp.float32),
        lax.psum(down_sum.astype(jnp.bfloat16), "replica").astype(jnp.float32),
    )
    gain_one, bias_one, weight_qkv, bias_qkv, weight_out = (
        lax.all_gather(ln1_gain, "shard", axis=0, tiled=True),
        lax.all_gather(ln1_bias, "shard", axis=0, tiled=True),
        lax.all_gather(qkv_weight, "shard", axis=0, tiled=True),
        lax.all_gather(qkv_bias, "shard", axis=0, tiled=True),
        lax.all_gather(out_weight, "shard", axis=0, tiled=True),
    )
    grad_middle_low = grad_middle.astype(jnp.bfloat16)
    out_weight_grad = jnp.einsum(
        "td,te->de", mixed, grad_middle_low, preferred_element_type=jnp.float32
    )
    grad_mixed = jnp.einsum(
        "te,de->td", grad_middle_low, weight_out, preferred_element_type=jnp.float32
    ).astype(jnp.bfloat16)
    grad_mixed = grad_mixed.reshape(sequences, length, HEADS, HEAD_DIM)
    probs_again = attention_probs(queries, keys, allowed, logsum)
    grad_values = jnp.einsum(
        "shlm,slhd->smhd",
        probs_again.astype(jnp.bfloat16),
        grad_mixed,
        preferred_element_type=jnp.float32,
    )
    grad_probs = jnp.einsum(
        "slhd,smhd->shlm", grad_mixed, values, preferred_element_type=jnp.float32
    )
    grad_scores = probs_again * (
        grad_probs - jnp.sum(probs_again * grad_probs, axis=-1, keepdims=True)
    )
    grad_scores = grad_scores.astype(jnp.bfloat16)
    grad_queries = (
        jnp.einsum("shlm,smhd->slhd", grad_scores, keys, preferred_element_type=jnp.float32) * scale
    )
    grad_keys = (
        jnp.einsum("shlm,slhd->smhd", grad_scores, queries, preferred_element_type=jnp.float32)
        * scale
    )
    grad_queries = rotate(grad_queries, cosine, -sine)
    grad_keys = rotate(grad_keys, cosine, -sine)
    grad_projected = (
        jnp.stack([grad_queries, grad_keys, grad_values], axis=2)
        .reshape(row_count, 3 * D)
        .astype(jnp.bfloat16)
    )
    qkv_bias_grad = jnp.sum(grad_projected.astype(jnp.float32), axis=0)
    qkv_weight_grad = jnp.einsum(
        "td,te->de", entry_one, grad_projected, preferred_element_type=jnp.float32
    )
    grad_entry_one = jnp.einsum(
        "te,de->td", grad_projected, weight_qkv, preferred_element_type=jnp.float32
    )
    ln1_gain_grad = jnp.sum(grad_entry_one * normed_one, axis=0)
    ln1_bias_grad = jnp.sum(grad_entry_one, axis=0)
    input_grad = grad_middle + norm_back(
        grad_entry_one, normed_one, inverse_one, gain_one.astype(jnp.float32)
    )
    gain_one_sum, bias_one_sum, qkv_sum, qkv_bias_sum, out_sum = (
        lax.psum_scatter(
            ln1_gain_grad.astype(jnp.bfloat16), "shard", scatter_dimension=0, tiled=True
        ).astype(jnp.float32),
        lax.psum_scatter(
            ln1_bias_grad.astype(jnp.bfloat16), "shard", scatter_dimension=0, tiled=True
        ).astype(jnp.float32),
        lax.psum_scatter(
            qkv_weight_grad.astype(jnp.bfloat16), "shard", scatter_dimension=0, tiled=True
        ).astype(jnp.float32),
        lax.psum_scatter(
            qkv_bias_grad.astype(jnp.bfloat16), "shard", scatter_dimension=0, tiled=True
        ).astype(jnp.float32),
        lax.psum_scatter(
            out_weight_grad.astype(jnp.bfloat16), "shard", scatter_dimension=0, tiled=True
        ).astype(jnp.float32),
    )
    gain_one_sum, bias_one_sum, qkv_sum, qkv_bias_sum, out_sum = (
        lax.psum(gain_one_sum.astype(jnp.bfloat16), "replica").astype(jnp.float32),
        lax.psum(bias_one_sum.astype(jnp.bfloat16), "replica").astype(jnp.float32),
        lax.psum(qkv_sum.astype(jnp.bfloat16), "replica").astype(jnp.float32),
        lax.psum(qkv_bias_sum.astype(jnp.bfloat16), "replica").astype(jnp.float32),
        lax.psum(out_sum.astype(jnp.bfloat16), "replica").astype(jnp.float32),
    )
    return (
        result.astype(jnp.bfloat16),
        input_grad.astype(jnp.bfloat16),
        gain_one_sum,
        bias_one_sum,
        qkv_sum,
        qkv_bias_sum,
        out_sum,
        gain_two_sum,
        bias_two_sum,
        gate_sum,
        up_sum,
        down_sum,
    )


def solution(mesh):
    return jax.shard_map(
        local,
        mesh=mesh,
        in_specs=(
            P(("replica", "shard"), None),
            P(("replica", "shard"), None),
            P(("replica", "shard"), None),
            P("shard"),
            P("shard"),
            P("shard", None),
            P("shard"),
            P("shard", None),
            P("shard"),
            P("shard"),
            P("shard", None),
            P("shard", None),
            P("shard", None),
        ),
        out_specs=(
            P(("replica", "shard"), None),
            P(("replica", "shard"), None),
            P("shard"),
            P("shard"),
            P("shard", None),
            P("shard"),
            P("shard", None),
            P("shard"),
            P("shard"),
            P("shard", None),
            P("shard", None),
            P("shard", None),
        ),
        check_vma=False,
    )
```

profile of v0, /device:TPU:1, one launch (start us, length us, event | category | flops | bytes accessed | tf_op | source)
XLA Modules:
  0.0 2700.9 jit_solution(18238874400672055347)
XLA Ops:
  14.1 145.3 %all-reduce.11 = (bf16[6144]{0:T(1024)(128)(2,1)S(1)}, bf16[2048]{0:T(1024)(128)(2,1)S(1)}, bf16[2048]{0:T(1024)(128)(2,1)S(1)}, bf16[2048]{0:T(1024)(128)(2,1)S(1)}, bf16[2048]{0:T(1024)(128)(2,1)S(1)}) all-reduce(bf16[6144]{0:T(1024)(128)(2,1)S(1)} %dynamic-update-slice.2, ...), channel_id=1, replica_groups=mesh['replica'=4,'shard'=32] {'shard'}, use_global_device_ids=true, to_apply=%add.2 | all-reduce | flops 14336 | bytes 57344
  162.4 131.1 %all-gather.6.cloned.1.call-done = bf16[2048,6144]{1,0:T(8,128)(2,1)} async-done(((bf16[64,6144]{1,0:T(8,128)(2,1)}), bf16[2048,6144]{1,0:T(8,128)(2,1)}) %all-gather.6.cloned.1.call-update) | async-done | bytes 25165840 | tf_op jit(solution)/shard_map/all_gather | solution.py:86
  293.6 13.5 convolution_add_fusion
  307.1 2.9 copy.46
  313.5 2.5 convolution_convert_fusion.7
  316.0 123.7 %all-gather.8.cloned.1.call-done = bf16[2048,2048]{1,0:T(8,128)(2,1)} async-done(((bf16[64,2048]{1,0:T(8,128)(2,1)}), bf16[2048,2048]{1,0:T(8,128)(2,1)}) %all-gather.8.cloned.1.call-update) | async-done | bytes 8388624 | tf_op jit(solution)/shard_map/all_gather | solution.py:88
  439.7 5.0 fusion.46
  446.8 270.7 %all-gather.12.cloned.1.call-done = bf16[2048,5632]{1,0:T(8,128)(2,1)} async-done(((bf16[64,5632]{1,0:T(8,128)(2,1)}), bf16[2048,5632]{1,0:T(8,128)(2,1)}) %all-gather.12.cloned.1.call-update) | async-done | bytes 23068688 | tf_op jit(solution)/shard_map/all_gather | solution.py:120
  717.4 12.8 fusion.48
  730.2 241.3 %all-gather.10.cloned.1.call-done = bf16[2048,5632]{1,0:T(8,128)(2,1)} async-done(((bf16[64,5632]{1,0:T(8,128)(2,1)}), bf16[2048,5632]{1,0:T(8,128)(2,1)}) %all-gather.10.cloned.1.call-update) | async-done | bytes 23068688 | tf_op jit(solution)/shard_map/all_gather | solution.py:119
  971.5 12.7 fusion.47
  984.2 241.3 %all-gather.14.cloned.1.call-done = bf16[5632,2048]{1,0:T(8,128)(2,1)} async-done(((bf16[176,2048]{1,0:T(8,128)(2,1)}), bf16[5632,2048]{1,0:T(8,128)(2,1)}) %all-gather.14.cloned.1.call-update) | async-done | bytes 23068688 | tf_op jit(solution)/shard_map/all_gather | solution.py:121
  1225.5 15.5 multiply_convert_fusion
  1241.0 13.0 fusion.49
  1254.1 14.2 multiply_reduce_fusion.1
  1271.3 5.6 convolution_convert_fusion.4
  1276.9 12.3 convolution_convert_fusion
  1289.3 12.4 convolution_convert_fusion.1
  1301.7 12.3 convolution_convert_fusion.2
  1314.5 7.5 convolution_convert_fusion.6
  1331.7 12.1 convolution_convert_fusion.3
  1345.4 85.0 %reduce-scatter.8.cloned.1.call-done = bf16[64,2048]{1,0:T(8,128)(2,1)} async-done(((bf16[2048,2048]{1,0:T(8,128)(2,1)}), bf16[64,2048]{1,0:T(8,128)(2,1)}) %reduce-scatter.8.cloned.1.call-update) | async-done | bytes 262160 | tf_op jit(solution)/shard_map/reduce_scatter | solution.py:259
  1430.4 276.7 %reduce-scatter.14.cloned.1.call-done = bf16[176,2048]{1,0:T(8,128)(2,1)} async-done(((bf16[5632,2048]{1,0:T(8,128)(2,1)}), bf16[176,2048]{1,0:T(8,128)(2,1)}) %reduce-scatter.14.cloned.1.call-update) | async-done | bytes 720912 | tf_op jit(solution)/shard_map/reduce_scatter | solution.py:180
  1707.1 254.5 %reduce-scatter.12.cloned.1.call-done = bf16[64,5632]{1,0:T(8,128)(2,1)} async-done(((bf16[2048,5632]{1,0:T(8,128)(2,1)}), bf16[64,5632]{1,0:T(8,128)(2,1)}) %reduce-scatter.12.cloned.1.call-update) | async-done | bytes 720912 | tf_op jit(solution)/shard_map/reduce_scatter | solution.py:177
  1961.6 254.6 %reduce-scatter.10.cloned.1.call-done = bf16[64,5632]{1,0:T(8,128)(2,1)} async-done(((bf16[2048,5632]{1,0:T(8,128)(2,1)}), bf16[64,5632]{1,0:T(8,128)(2,1)}) %reduce-scatter.10.cloned.1.call-update) | async-done | bytes 720912 | tf_op jit(solution)/shard_map/reduce_scatter | solution.py:174
  2216.2 276.2 %reduce-scatter.6.cloned.1.call-done = bf16[64,6144]{1,0:T(8,128)(2,1)} async-done(((bf16[2048,6144]{1,0:T(8,128)(2,1)}), bf16[64,6144]{1,0:T(8,128)(2,1)}) %reduce-scatter.6.cloned.1.call-update) | async-done | bytes 786448 | tf_op jit(solution)/shard_map/reduce_scatter | solution.py:253
  2492.5 14.7 fusion.19
  2507.2 127.1 %all-reduce.10 = (bf16[2048]{0:T(1024)(128)(2,1)S(1)}, bf16[2048]{0:T(1024)(128)(2,1)S(1)}, bf16[6144]{0:T(1024)(128)(2,1)S(1)}, bf16[2048]{0:T(1024)(128)(2,1)S(1)}, bf16[2048]{0:T(1024)(128)(2,1)S(1)}) all-reduce(bf16[2048]{0:T(1024)(128)(2,1)S(1)} %get-tuple-element.14, ...), channel_id=2, replica_groups=mesh['replica'=4,'shard'=32] {'shard'}, use_global_device_ids=true, to_apply=%region_13.14.clone | all-reduce | flops 14336 | bytes 57344
  2634.7 34.6 %all-reduce.12 = (bf16[64]{0:T(256)(128)(2,1)S(1)}, bf16[64]{0:T(256)(128)(2,1)S(1)}, bf16[192]{0:T(256)(128)(2,1)S(1)}, bf16[64]{0:T(256)(128)(2,1)S(1)}, bf16[64]{0:T(256)(128)(2,1)S(1)}) all-reduce(bf16[64]{0:T(256)(128)(2,1)S(1)} %dynamic-slice.6, ...), channel_id=1, replica_groups=mesh['replica'=4,'shard'=32] {'replica'}, use_global_device_ids=true, to_apply=%region_14.15 | all-reduce | flops 448 | bytes 1792 | tf_op jit(solution)/shard_map/psum | solution.py:264
  2671.9 2.8 fusion.18
  2674.7 11.5 fusion.1
  2688.1 2.4 convert_element_type.245
  (184 shorter events, 36.0 us)
Async XLA Ops:
  7.2 5.4 copy-start.40
  7.2 5.6 copy-start.42
  7.2 5.9 copy-start.43
  7.2 6.1 copy-start.44
  7.2 6.3 copy-start.45
  7.2 6.6 copy-start.46
  7.3 153.3 %copy-start = (bf16[128,2048]{1,0:T(8,128)(2,1)S(1)}, bf16[128,2048]{1,0:T(8,128)(2,1)}, u32[]{:S(2)}) copy-start(bf16[128,2048]{1,0:T(8,128)(2,1)} %param.13) | copy-start | bytes 1572868
  7.3 286.3 %all-gather.6.cloned.1.call-start = ((), (), s32[]{:S(2)}) async-start(), calls=%async_computation.5 | async-start | bytes 25952256 | tf_op jit(solution)/shard_map/all_gather | solution.py:86
  8.0 431.7 %all-gather.8.cloned.1.call-start = ((), (), s32[]{:S(2)}) async-start(), calls=%async_computation.6 | async-start | bytes 8650752 | tf_op jit(solution)/shard_map/all_gather | solution.py:88
  8.7 708.7 %all-gather.12.cloned.1.call-start = ((), (), s32[]{:S(2)}) async-start(), calls=%async_computation.8 | async-start | bytes 23789568 | tf_op jit(solution)/shard_map/all_gather | solution.py:120
  9.5 962.0 %all-gather.10.cloned.1.call-start = ((), (), s32[]{:S(2)}) async-start(), calls=%async_computation.7 | async-start | bytes 23789568 | tf_op jit(solution)/shard_map/all_gather | solution.py:119
  10.1 1215.4 %all-gather.14.cloned.1.call-start = ((), (), s32[]{:S(2)}) async-start(), calls=%async_computation.9 | async-start | bytes 23789568 | tf_op jit(solution)/shard_map/all_gather | solution.py:121
  10.6 1419.7 %reduce-scatter.8.cloned.1.call-start = ((), (), s32[]{:S(2)}) async-start(), calls=%async_computation.11 | async-start | bytes 8650752 | tf_op jit(solution)/shard_map/reduce_scatter | solution.py:259
  160.7 146.4 %copy-start.27 = (f32[128]{0:T(128)}, f32[128]{0:T(128)S(1)}, u32[]{:S(2)}) copy-start(f32[128]{0:T(128)S(1)} %broadcast_multiply_fusion.5) | copy-start | bytes 1540
  161.0 146.1 %copy-start.30 = (f32[128]{0:T(128)}, f32[128]{0:T(128)S(1)}, u32[]{:S(2)}) copy-start(f32[128]{0:T(128)S(1)} %add_rsqrt_fusion.1) | copy-start | bytes 1540
  161.7 148.5 %copy-start.25 = (f32[128,8]{0,1:T(8,128)}, f32[128,8]{0,1:T(8,128)S(1)}, u32[]{:S(2)}) copy-start(f32[128,8]{0,1:T(8,128)S(1)} %get-tuple-element.61) | copy-start | bytes 12292
  439.7 6.0 copy-start.21
  439.7 6.0 copy-start.29
  1241.0 13.1 copy-start.4
  1241.0 13.1 copy-start.22
  1241.0 13.1 copy-start.37
  1241.0 13.1 copy-start.39
  1276.9 430.2 %reduce-scatter.14.cloned.1.call-start = ((), (), s32[]{:S(2)}) async-start(), calls=%async_computation.14 | async-start | bytes 23789568 | tf_op jit(solution)/shard_map/reduce_scatter | solution.py:180
  1289.2 672.4 %reduce-scatter.12.cloned.1.call-start = ((), (), s32[]{:S(2)}) async-start(), calls=%async_computation.13 | async-start | bytes 23789568 | tf_op jit(solution)/shard_map/reduce_scatter | solution.py:177
  1301.7 914.5 %reduce-scatter.10.cloned.1.call-start = ((), (), s32[]{:S(2)}) async-start(), calls=%async_computation.12 | async-start | bytes 23789568 | tf_op jit(solution)/shard_map/reduce_scatter | solution.py:174
  1314.0 1178.4 %reduce-scatter.6.cloned.1.call-start = ((), (), s32[]{:S(2)}) async-start(), calls=%async_computation.10 | async-start | bytes 25952256 | tf_op jit(solution)/shard_map/reduce_scatter | solution.py:253
  1343.9 1342.4 %all-reduce.16.cloned.1.call-start = ((), (), s32[]{:S(2)}) async-start(), calls=%async_computation.15 | async-start | bytes 6422528 | tf_op jit(solution)/shard_map/psum | solution.py:266
  2492.4 14.8 copy-start.34
  2492.5 14.8 copy-start.35
  2507.1 167.6 %copy-start.5 = (bf16[128,5632]{1,0:T(8,128)(2,1)S(1)}, bf16[128,5632]{1,0:T(8,128)(2,1)}, u32[]{:S(2)}) copy-start(bf16[128,5632]{1,0:T(8,128)(2,1)} %get-tuple-element.44) | copy-start | bytes 4325380
  2686.2 5.5 copy-start.11
  2688.1 4.8 copy-start.10
  (26 other events, 39.4 us)
Sparse Core Ops, SparseCore 0:
  9.7 283.7 all-gather.5
  295.2 144.4 all-gather.7
  441.4 276.0 all-gather.11
  718.9 252.4 all-gather.9
  973.0 252.4 all-gather.13
  1277.0 153.3 reduce-scatter.7
  1432.8 274.2 reduce-scatter.13
  1709.5 252.0 reduce-scatter.11
  1964.0 252.1 reduce-scatter.9
  2218.4 273.9 reduce-scatter.5
  2495.3 75.1 all-reduce.15
where the time goes:
time: 2710 us; the launch traced here: 2700 us
  waiting for transfers between devices  2160 us (80%)
  blocking collectives  307 us (11%)
  matrix products  182 us (7%)
    reduce_scatter x1, waiting for transfers between devices, local(): lax.psum_scatter(down_weight_grad.astype(jnp.bfloat16), 'shard', scatter_...  277 us
    reduce_scatter x1, waiting for transfers between devices, local(): lax.psum_scatter(qkv_weight_grad.astype(jnp.bfloat16), 'shard', scatter_d...  276 us
    unnamed x2, blocking collectives  272 us
    all_gather x1, waiting for transfers between devices, local(): lax.all_gather(up_weight, 'shard', axis=0, tiled=True)  271 us
    reduce_scatter x1, waiting for transfers between devices, local(): lax.psum_scatter(gate_weight_grad.astype(jnp.bfloat16), 'shard', scatter_...  255 us
    reduce_scatter x1, waiting for transfers between devices, local(): lax.psum_scatter(up_weight_grad.astype(jnp.bfloat16), 'shard', scatter_di...  255 us
    all_gather x1, waiting for transfers between devices, local(): lax.all_gather(down_weight, 'shard', axis=0, tiled=True)  241 us
    all_gather x1, waiting for transfers between devices, local(): lax.all_gather(gate_weight, 'shard', axis=0, tiled=True)  241 us
  transfers between devices with their start and end apart: 11, of which 10 were waited for; matrix products, arithmetic and copies ran while one was open for 6% of the time, Pallas kernels for 0%

commit v1 on v0

v1 whole, which is shorter than its diff:
```python
import functools
import jax, jax.numpy as jnp
from jax import lax
from jax.sharding import PartitionSpec as P, Mesh
from jax.experimental import pallas as pl
from jax.experimental.pallas import tpu as pltpu

AXES = ("xh", "c", "z", "xl", "y")


class Place:
    def __init__(self):
        self.xh, self.c, self.z, self.xl, self.y = (lax.axis_index(a) for a in AXES)
        self.x = self.xh * 2 + self.xl

    def at(self, dx=0, dy=0, dz=0, dc=0):
        x = lax.rem(self.x + dx + 4, 4) if dx else self.x
        return (
            x // 2 if dx else self.xh,
            lax.rem(self.c + dc, 2) if dc else self.c,
            lax.rem(self.z + dz + 4, 4) if dz else self.z,
            lax.rem(x, 2) if dx else self.xl,
            lax.rem(self.y + dy + 4, 4) if dy else self.y,
        )


def barrier(targets):
    sem = pltpu.get_barrier_semaphore()
    for target in targets:
        pl.semaphore_signal(sem, inc=1, device_id=target, device_id_type=pl.DeviceIdType.MESH)
    pl.semaphore_wait(sem, len(targets))


class Copies:
    def __init__(self, send, recv):
        self.send, self.recv, self.used, self.all = send, recv, 0, []

    def push(self, src, dst, target):
        copy = pltpu.make_async_remote_copy(
            src_ref=src, dst_ref=dst, send_sem=self.send.at[self.used],
            recv_sem=self.recv.at[self.used], device_id=target, device_id_type=pl.DeviceIdType.MESH)
        self.used += 1
        self.all.append(copy)
        copy.start()
        return copy

    def finish(self):
        for copy in self.all:
            copy.wait_send()


N_REMOTE, N_LOCAL = 96, 16


def gather_kernel(tok, cot, seg, wq, sm, wg, wu, wo, wd,
                  toks, cots, segs, gq, gs, gg, gu, go, gd, send, recv, lsem):
    p = Place()
    barrier([p.at(dy=d) for d in (1, 2, 3)] + [p.at(dz=d) for d in (1, 2, 3)] + [p.at(dx=1), p.at(dx=-1), p.at(dc=1)])
    cp = Copies(send, recv)
    locals_ = []

    def local(src, dst):
        copy = pltpu.make_async_copy(src, dst, lsem.at[len(locals_)])
        copy.start()
        locals_.append(copy)
        return copy

    x1, x3, sib = p.at(dx=1), p.at(dx=-1), p.at(dc=1)
    half = pl.ds(pl.multiple_of(p.c * 32, 32), 32)
    cols = pl.ds(pl.multiple_of(p.c * 1024, 1024), 1024)
    acts = []

    def share(src, dst):
        local(src, dst.at[p.y])
        for d in (1, 3, 2):
            acts.append(cp.push(src, dst.at[p.y], p.at(dy=d)))

    rows = [dict(src=s, g=g) for s, g in ((wq, gq), (sm, gs), (wg, gg), (wu, gu))]
    plane = [dict(src=s, g=g, cut=c) for s, g, c in ((wo, go, 32), (wd, gd, 96))]

    def stage_y(a):
        a["local"] = local(a["src"].at[p.y, half], a["g"].at[p.z, p.xl, p.y, half])
        a["y"] = [cp.push(a["src"].at[lax.rem(p.y + d, 4), half], a["g"].at[p.z, p.xl, p.y, half], p.at(dy=d)) for d in (1, 3, 2)]

    def stage_z(a):
        if "cut" in a:
            a["local"] = local(a["src"].at[:, cols], a["g"].at[p.z, p.xl, :, cols])
            a["z"] = [cp.push(a["src"].at[:, cols], a["g"].at[p.z, p.xl, :, cols], p.at(dz=d)) for d in (1, 3, 2)]
        else:
            a["local"].wait()
            for c in a["y"]:
                c.wait_recv()
            a["z"] = [cp.push(a["g"].at[p.z, p.xl, :, half], a["g"].at[p.z, p.xl, :, half], p.at(dz=d)) for d in (1, 3, 2)]

    def parts(a, xl):
        g = a["g"]
        if "cut" in a:
            k = a["cut"]
            r = g.shape[2]
            return g.at[:, xl, 0:k, cols], g.at[:, xl, k:r, cols], g.at[:, xl, :, cols]
        return g.at[:, xl, 0:2, half], g.at[:, xl, 2:4, half], g.at[:, xl, :, half]

    def stage_x(a):
        if "cut" in a:
            a["local"].wait()
        for c in a["z"]:
            c.wait_recv()
        lo, hi, full = parts(a, p.xl)
        a["x"] = [cp.push(lo, lo, x1), cp.push(hi, hi, x3)]
        a["c"] = [cp.push(full, full, sib)]

    def stage_c(a):
        lo, hi, full = parts(a, 1 - p.xl)
        a["x"][0].wait_recv()
        a["c"].append(cp.push(lo, lo, sib))
        a["x"][1].wait_recv()
        a["c"].append(cp.push(hi, hi, sib))

    q, s, g, u = rows
    o, d = plane
    stage_y(q); stage_y(s)
    share(tok, toks)
    share(seg, segs)
    stage_y(g); stage_y(u)
    share(cot, cots)
    stage_z(q); stage_z(s); stage_z(o)
    stage_z(g); stage_z(u); stage_z(d)
    for a in (q, s, o, g, u, d):
        stage_x(a)
    for a in (q, s, o, g, u, d):
        stage_c(a)
    for c in acts:
        c.wait_recv()
    for a in (q, s, o, g, u, d):
        for c in a["c"]:
            c.wait_recv()
    cp.finish()
    for copy in locals_[:]:
        if not any(copy is a["local"] for a in rows + plane):
            copy.wait()


def gather(tok, cot, seg, wq, sm, wg, wu, wo, wd):
    bf = jnp.bfloat16
    S = jax.ShapeDtypeStruct
    hbm = pl.BlockSpec(memory_space=pl.ANY)
    outs = (S((4, 128, 2048), bf), S((4, 128, 2048), bf), S((4, 8, 128), jnp.float32),
            S((4, 2, 4, 64, 1536), bf), S((4, 2, 4, 64, 128), bf), S((4, 2, 4, 64, 1408), bf), S((4, 2, 4, 64, 1408), bf),
            S((4, 2, 64, 2048), bf), S((4, 2, 176, 2048), bf))
    return pl.pallas_call(
        gather_kernel, out_shape=outs, in_specs=[hbm] * 9, out_specs=(hbm,) * 9,
        scratch_shapes=[pltpu.SemaphoreType.DMA((N_REMOTE,)), pltpu.SemaphoreType.DMA((N_REMOTE,)), pltpu.SemaphoreType.DMA((N_LOCAL,))],
        compiler_params=pltpu.CompilerParams(collective_id=1, has_side_effects=True),
        name="gather",
    )(tok, cot, seg, wq, sm, wg, wu, wo, wd)


def add_into(out, parts):
    total = parts[0][...].astype(jnp.float32)
    for part in parts[1:]:
        total = total + part[...].astype(jnp.float32)
    out[...] = total.astype(out.dtype)


class Reduce:
    def __init__(self, p, cp, source, bufs, out, cut=None):
        self.p, self.cp, self.source, self.out, self.cut = p, cp, source, out, cut
        self.h, self.rc, self.rx, self.rz, self.rxh, self.ky = bufs
        if cut is None:
            self.mine = lambda ref, c: ref.at[:, :, :, pl.ds(pl.multiple_of(c * 32, 32), 32)]
        else:
            self.mine = lambda ref, c: ref.at[:, :, :, pl.ds(pl.multiple_of(c * 1024, 1024), 1024)]

    def start(self, sem):
        p = self.p
        self.load = pltpu.make_async_copy(self.mine(self.source, p.c), self.h, sem)
        self.load.start()
        self.core = self.cp.push(self.mine(self.source, 1 - p.c), self.rc, p.at(dc=1))

    def blocks(self, ref):
        return (ref.shape[-2] if self.cut is not None else ref.shape[-3])

    def stage_x(self):
        p, h, rc = self.p, self.h, self.rc
        self.load.wait()
        self.core.wait_recv()

        def foreign(i, _):
            add_into(h.at[i, 1 - p.xl], (h.at[i, 1 - p.xl], rc.at[i, 1 - p.xl]))
            return 0

        lax.fori_loop(0, 4, foreign, 0)
        k, n = (2, 4) if self.cut is None else (self.cut, h.shape[2])
        self.x = [
            self.cp.push(h.at[:, 1 - p.xl, 0:k], self.rx.at[:, 0:k], p.at(dx=1)),
            self.cp.push(h.at[:, 1 - p.xl, k:n], self.rx.at[:, k:n], p.at(dx=-1)),
        ]

    def stage_z(self):
        p, h, rc, rx = self.p, self.h, self.rc, self.rx
        for c in self.x:
            c.wait_recv()

        def own(i, _):
            add_into(h.at[i, p.xl], (h.at[i, p.xl], rc.at[i, p.xl], rx.at[i]))
            return 0

        lax.fori_loop(0, 4, own, 0)
        self.zs = [self.cp.push(h.at[lax.rem(p.z + d, 4), p.xl], self.rz.at[d - 1], p.at(dz=d)) for d in (1, 3, 2)]

    def stage_xh(self):
        p, h, rz = self.p, self.h, self.rz
        for c in self.zs:
            c.wait_recv()
        add_into(h.at[p.z, p.xl], (h.at[p.z, p.xl], rz.at[0], rz.at[1], rz.at[2]))
        self.xh = self.cp.push(h.at[p.z, p.xl], self.rxh, p.at(dx=2))

    def stage_y(self, sem):
        p = self.p
        self.xh.wait_recv()
        add_into(self.ky, (self.h.at[p.z, p.xl], self.rxh))
        if self.cut is None:
            half = pl.ds(pl.multiple_of(p.c * 32, 32), 32)
            self.own = pltpu.make_async_copy(self.ky.at[p.y], self.out.at[p.y, half], sem)
            self.own.start()
            self.ys = [
                self.cp.push(self.ky.at[lax.rem(p.y + d, 4)], self.out.at[p.y, half], p.at(dy=d)) for d in (1, 3, 2)
            ]
        else:
            cols = pl.ds(pl.multiple_of(p.c * 1024, 1024), 1024)
            self.own = pltpu.make_async_copy(self.ky, self.out.at[:, cols], sem)
            self.own.start()
            self.ys = [self.cp.push(self.ky, self.out.at[:, cols], p.at(dc=1))]

    def stage_end(self):
        p = self.p
        for c in self.ys:
            c.wait_recv()
        self.own.wait()
        if self.cut is None:
            half = pl.ds(pl.multiple_of(p.c * 32, 32), 32)
            self.last = self.cp.push(self.out.at[:, half], self.out.at[:, half], p.at(dc=1))
        else:
            self.last = None

    def finish(self):
        if self.last is not None:
            self.last.wait_recv()


def reduce_scratch(shape, plane):
    bf = jnp.bfloat16
    if plane:
        rows = shape[2]
        tail = (rows, 1024)
    else:
        tail = (4, 32, shape[-1])
    return [pltpu.VMEM((4, 2) + tail, bf), pltpu.VMEM((4, 2) + tail, bf), pltpu.VMEM((4,) + tail, bf),
            pltpu.VMEM((3,) + tail, bf), pltpu.VMEM(tail, bf), pltpu.VMEM(tail, bf)]


def run_reduces(reduces, sems):
    for r in reduces:
        r.stage_x()
    for r in reduces:
        r.stage_z()
    for r in reduces:
        r.stage_xh()
    for i, r in enumerate(reduces):
        r.stage_y(sems.at[i])
    for r in reduces:
        r.stage_end()
    for r in reduces:
        r.finish()


def peers(p):
    return [p.at(dy=d) for d in (1, 2, 3)] + [p.at(dz=d) for d in (1, 2, 3)] + [p.at(dx=d) for d in (1, 2, -1)] + [p.at(dc=1)]


ROWS = 16


def middle_kernel(part, tok, gains, mid, ents, recv_a, own, ent, send, recv, lsem):
    p = Place()
    barrier([p.at(dy=d) for d in (1, 2, 3)])
    cp = Copies(send, recv)
    load = pltpu.make_async_copy(part.at[p.y], own, lsem.at[0])
    load.start()
    ins = [cp.push(part.at[lax.rem(p.y + d, 4)], recv_a.at[d - 1], p.at(dy=d)) for d in (1, 3, 2)]
    load.wait()
    for c in ins:
        c.wait_recv()

    def block(i, _):
        r = pl.ds(pl.multiple_of(i * ROWS, ROWS), ROWS)
        f = jnp.float32
        m = tok[r].astype(f) + own[r].astype(f) + recv_a[0, r].astype(f) + recv_a[1, r].astype(f) + recv_a[2, r].astype(f)
        mid[r] = m
        m = m - jnp.mean(m, axis=-1, keepdims=True)
        m = m * lax.rsqrt(jnp.mean(m * m, axis=-1, keepdims=True) + norm_epsilon)
        ent[r] = (m * gains[0:1, :] + gains[1:2, :]).astype(jnp.bfloat16)
        return 0

    lax.fori_loop(0, 128 // ROWS, block, 0)
    keep = pltpu.make_async_copy(ent, ents.at[p.y], lsem.at[0])
    keep.start()
    outs = [cp.push(ent, ents.at[p.y], p.at(dy=d)) for d in (1, 3, 2)]
    keep.wait()
    for c in outs:
        c.wait_recv()
    cp.finish()


def middle_step(part, tok, gains):
    bf = jnp.bfloat16
    S = jax.ShapeDtypeStruct
    hbm, vm = pl.BlockSpec(memory_space=pl.ANY), pl.BlockSpec(memory_space=pltpu.VMEM)
    return pl.pallas_call(
        middle_kernel, out_shape=(S((128, 2048), jnp.float32), S((4, 128, 2048), bf)),
        in_specs=[hbm, vm, vm], out_specs=(vm, hbm),
        scratch_shapes=[pltpu.VMEM((3, 128, 2048), bf), pltpu.VMEM((128, 2048), bf), pltpu.VMEM((128, 2048), bf),
                        pltpu.SemaphoreType.DMA((6,)), pltpu.SemaphoreType.DMA((6,)), pltpu.SemaphoreType.DMA((1,))],
        compiler_params=pltpu.CompilerParams(collective_id=2, has_side_effects=True, vmem_limit_bytes=32 * 2**20),
        name="middle_step",
    )(part, tok, gains)


def back_kernel(gpart, rpart, mid, cot, gains, dg, du, dd,
                act, gmid, gmls, sums, og, ou, od,
                recv_g, recv_r, own_g, own_r, low, send, recv, lsem, *bufs):
    p = Place()
    f = jnp.float32
    barrier(peers(p))
    cp = Copies(send, recv)
    loads = [pltpu.make_async_copy(gpart.at[p.y], own_g, lsem.at[0]), pltpu.make_async_copy(rpart.at[p.y], own_r, lsem.at[1])]
    for load in loads:
        load.start()
    gs = [cp.push(gpart.at[lax.rem(p.y + d, 4)], recv_g.at[d - 1], p.at(dy=d)) for d in (1, 3, 2)]
    reduces = [Reduce(p, cp, dd, bufs[0:6], od, 96), Reduce(p, cp, dg, bufs[6:12], og), Reduce(p, cp, du, bufs[12:18], ou)]
    for i, r in enumerate(reduces):
        r.start(lsem.at[2 + i])
    for load in loads:
        load.wait()
    for c in gs:
        c.wait_recv()
    sums[...] = jnp.zeros_like(sums)

    def block(i, _):
        r = pl.ds(pl.multiple_of(i * ROWS, ROWS), ROWS)
        g = own_g[r].astype(f) + recv_g[0, r].astype(f) + recv_g[1, r].astype(f) + recv_g[2, r].astype(f)
        m = mid[r]
        m = m - jnp.mean(m, axis=-1, keepdims=True)
        inv = lax.rsqrt(jnp.mean(m * m, axis=-1, keepdims=True) + norm_epsilon)
        m = m * inv
        sums[0:1] += jnp.sum(g * m, axis=0, keepdims=True)
        sums[1:2] += jnp.sum(g, axis=0, keepdims=True)
        e = g * gains[0:1, :]
        out = cot[r].astype(f) + inv * (e - jnp.mean(e, axis=-1, keepdims=True) - m * jnp.mean(e * m, axis=-1, keepdims=True))
        gmid[r] = out
        low[r] = out.astype(jnp.bfloat16)
        return 0

    lax.fori_loop(0, 128 // ROWS, block, 0)
    keep = pltpu.make_async_copy(low, gmls.at[p.y], lsem.at[0])
    keep.start()
    ls = [cp.push(low, gmls.at[p.y], p.at(dy=d)) for d in (1, 3, 2)]
    rs = [cp.push(rpart.at[lax.rem(p.y + d, 4)], recv_r.at[d - 1], p.at(dy=d)) for d in (1, 3, 2)]
    run_reduces(reduces, lsem.at[pl.ds(5, 3)])
    for c in rs:
        c.wait_recv()

    def final(i, _):
        r = pl.ds(pl.multiple_of(i * ROWS, ROWS), ROWS)
        act[r] = (mid[r] + own_r[r].astype(f) + recv_r[0, r].astype(f) + recv_r[1, r].astype(f) + recv_r[2, r].astype(f)).astype(jnp.bfloat16)
        return 0

    lax.fori_loop(0, 128 // ROWS, final, 0)
    keep.wait()
    for c in ls:
        c.wait_recv()
    cp.finish()


def back_step(gpart, rpart, mid, cot, gains, dg, du, dd):
    bf = jnp.bfloat16
    S = jax.ShapeDtypeStruct
    hbm, vm = pl.BlockSpec(memory_space=pl.ANY), pl.BlockSpec(memory_space=pltpu.VMEM)
    return pl.pallas_call(
        back_kernel,
        out_shape=(S((128, 2048), bf), S((128, 2048), jnp.float32), S((4, 128, 2048), bf), S((8, 2048), jnp.float32),
                   S((4, 64, 1408), bf), S((4, 64, 1408), bf), S((176, 2048), bf)),
        in_specs=[hbm, hbm, vm, vm, vm, hbm, hbm, hbm], out_specs=(vm, vm, hbm, vm, hbm, hbm, hbm),
        scratch_shapes=[pltpu.VMEM((3, 128, 2048), bf), pltpu.VMEM((3, 128, 2048), bf), pltpu.VMEM((128, 2048), bf),
                        pltpu.VMEM((128, 2048), bf), pltpu.VMEM((128, 2048), bf),
                        pltpu.SemaphoreType.DMA((48,)), pltpu.SemaphoreType.DMA((48,)), pltpu.SemaphoreType.DMA((8,))]
        + reduce_scratch(dd.shape, True) + reduce_scratch(dg.shape, False) + reduce_scratch(du.shape, False),
        compiler_params=pltpu.CompilerParams(collective_id=3, has_side_effects=True, vmem_limit_bytes=56 * 2**20),
        name="back_step",
    )(gpart, rpart, mid, cot, gains, dg, du, dd)


def last_kernel(gpart, tok, gmid, gains, rows, dq, do,
                ing, oq, os, oo,
                recv_g, own_g, wide, small, send, recv, lsem, *bufs):
    p = Place()
    f = jnp.float32
    barrier(peers(p))
    cp = Copies(send, recv)
    load = pltpu.make_async_copy(gpart.at[p.y], own_g, lsem.at[0])
    load.start()
    gs = [cp.push(gpart.at[lax.rem(p.y + d, 4)], recv_g.at[d - 1], p.at(dy=d)) for d in (1, 3, 2)]
    rq = Reduce(p, cp, dq, bufs[0:6], oq)
    ro = Reduce(p, cp, do, bufs[6:12], oo, 32)
    rs = Reduce(p, cp, small, bufs[12:18], os)
    rq.start(lsem.at[1])
    ro.start(lsem.at[2])
    wide[...] = jnp.zeros_like(wide)
    wide[0:8] = rows[...]
    load.wait()
    for c in gs:
        c.wait_recv()

    def block(i, _):
        r = pl.ds(pl.multiple_of(i * ROWS, ROWS), ROWS)
        g = own_g[r].astype(f) + recv_g[0, r].astype(f) + recv_g[1, r].astype(f) + recv_g[2, r].astype(f)
        m = tok[r].astype(f)
        m = m - jnp.mean(m, axis=-1, keepdims=True)
        inv = lax.rsqrt(jnp.mean(m * m, axis=-1, keepdims=True) + norm_epsilon)
        m = m * inv
        wide[0:1] += jnp.sum(g * m, axis=0, keepdims=True)
        wide[1:2] += jnp.sum(g, axis=0, keepdims=True)
        e = g * gains[0:1, :]
        out = gmid[r] + inv * (e - jnp.mean(e, axis=-1, keepdims=True) - m * jnp.mean(e * m, axis=-1, keepdims=True))
        ing[r] = out.astype(jnp.bfloat16)
        return 0

    lax.fori_loop(0, 128 // ROWS, block, 0)
    for i in range(16):
        z, xl, y = i // 4, (i // 2) % 2, (i % 2) * 2
        piece = jnp.transpose(wide[:, i * 128:(i + 1) * 128]).astype(jnp.bfloat16)
        small[z, xl, y] = piece[0:64]
        small[z, xl, y + 1] = piece[64:128]
    rs.start(lsem.at[3])
    run_reduces([ro, rq, rs], lsem.at[pl.ds(4, 3)])
    cp.finish()


def last_step(gpart, tok, gmid, gains, rows, dq, do):
    bf = jnp.bfloat16
    S = jax.ShapeDtypeStruct
    hbm, vm = pl.BlockSpec(memory_space=pl.ANY), pl.BlockSpec(memory_space=pltpu.VMEM)
    return pl.pallas_call(
        last_kernel,
        out_shape=(S((128, 2048), bf), S((4, 64, 1536), bf), S((4, 64, 128), bf), S((64, 2048), bf)),
        in_specs=[hbm, vm, vm, vm, vm, hbm, hbm], out_specs=(vm, hbm, hbm, hbm),
        scratch_shapes=[pltpu.VMEM((3, 128, 2048), bf), pltpu.VMEM((128, 2048), bf), pltpu.VMEM((128, 2048), jnp.float32),
                        pltpu.VMEM((4, 2, 4, 64, 128), bf),
                        pltpu.SemaphoreType.DMA((48,)), pltpu.SemaphoreType.DMA((48,)), pltpu.SemaphoreType.DMA((8,))]
        + reduce_scratch(dq.shape, False) + reduce_scratch(do.shape, True) + reduce_scratch((4, 2, 4, 64, 128), False),
        compiler_params=pltpu.CompilerParams(collective_id=4, has_side_effects=True, vmem_limit_bytes=56 * 2**20),
        name="last_step",
    )(gpart, tok, gmid, gains, rows, dq, do)


norm_epsilon = 1e-05
masked_score = -1000000000.0
HEADS = 8
HEAD_DIM = 64
ROT = 16


def layout(segments):
    length = segments.shape[1]
    same = segments[:, :, None] == segments[:, None, :]
    query_index = lax.broadcasted_iota(jnp.int32, (length, length), 0)
    key_index = lax.broadcasted_iota(jnp.int32, (length, length), 1)
    allowed = same & (key_index <= query_index)[None]
    places = jnp.sum((same & (key_index < query_index)[None]).astype(jnp.int32), axis=-1).astype(jnp.float32)
    half_rot = ROT // 2
    freqs = 10000.0 ** (-(jnp.arange(half_rot, dtype=jnp.float32) * 2.0) / ROT)
    angles = places[:, :, None, None] * freqs
    return (allowed[:, None], jnp.cos(angles), jnp.sin(angles))


def rotate(values, cosine, sine):
    half_rot = ROT // 2
    first = values[..., :half_rot]
    second = values[..., half_rot:ROT]
    return jnp.concatenate(
        [first * cosine - second * sine, second * cosine + first * sine, values[..., ROT:]], axis=-1
    )


def local(tokens, segment_ids, cotangent, ln1_gain, ln1_bias, qkv_weight, qkv_bias, out_weight,
          ln2_gain, ln2_bias, gate_weight, up_weight, down_weight):
    f, bf = jnp.float32, jnp.bfloat16
    scale = HEAD_DIM ** (-0.5)
    y = lax.axis_index("y")
    wq = qkv_weight.reshape(64, 3, 8, 4, 64).transpose(3, 0, 1, 2, 4).reshape(4, 64, 1536)
    wg = gate_weight.reshape(64, 8, 4, 176).transpose(2, 0, 1, 3).reshape(4, 64, 1408)
    wu = up_weight.reshape(64, 8, 4, 176).transpose(2, 0, 1, 3).reshape(4, 64, 1408)
    small = jnp.concatenate([jnp.stack([ln1_gain, ln1_bias, ln2_gain, ln2_bias], axis=1), qkv_bias.reshape(3, 64).T,
                             jnp.zeros((64, 121), bf)], axis=1)
    small = jnp.broadcast_to(small[None], (4, 64, 128))
    seg = jnp.broadcast_to(segment_ids.astype(f), (8, 128))
    toks, cots, segs, gq, gs, gg, gu, go, gd = gather(tokens, cotangent, seg, wq, small, wg, wu, out_weight, down_weight)
    gq, gg, gu = gq.reshape(2048, 1536), gg.reshape(2048, 1408), gu.reshape(2048, 1408)
    go, gd = go.reshape(512, 2048), gd.reshape(1408, 2048)
    gs = gs.reshape(2048, 128)[:, :8].astype(f).T
    bias = gs[4:7].reshape(3, 32, 64).transpose(1, 0, 2).reshape(3, 8, 4, 64)
    bias = lax.dynamic_index_in_dim(bias, y, 2, False).reshape(1536)
    gains_two = jnp.concatenate([gs[2:4], jnp.zeros((6, 2048), f)])
    allowed, cosine, sine = layout(segs[:, 0, :])

    x = toks.reshape(512, 2048).astype(f)
    x = x - jnp.mean(x, axis=-1, keepdims=True)
    x = x * lax.rsqrt(jnp.mean(x * x, axis=-1, keepdims=True) + norm_epsilon)
    entry_one = (x * gs[0] + gs[1]).astype(bf)
    projected = jnp.dot(entry_one, gq, preferred_element_type=f) + bias
    projected = projected.reshape(4, 128, 3, HEADS, HEAD_DIM)
    queries = rotate(projected[:, :, 0], cosine, sine).astype(bf)
    keys = rotate(projected[:, :, 1], cosine, sine).astype(bf)
    values = projected[:, :, 2].astype(bf)
    scores = jnp.einsum("slhd,smhd->shlm", queries, keys, preferred_element_type=f) * scale
    scores = jnp.where(allowed, scores, masked_score)
    peak = jnp.max(scores, axis=-1, keepdims=True)
    expos = jnp.exp(scores - peak)
    probs = expos / jnp.sum(expos, axis=-1, keepdims=True)
    mixed = jnp.einsum("shlm,smhd->slhd", probs.astype(bf), values, preferred_element_type=f)
    mixed = mixed.reshape(512, 512).astype(bf)
    out_part = jnp.dot(mixed, go, preferred_element_type=f).astype(bf).reshape(4, 128, 2048)
    mid, ents = middle_step(out_part, tokens, gains_two)

    entry_two = ents.reshape(512, 2048)
    gate = jnp.dot(entry_two, gg, preferred_element_type=f)
    upward = jnp.dot(entry_two, gu, preferred_element_type=f)
    sigmoid = jax.nn.sigmoid(gate)
    hidden = (gate * sigmoid * upward).astype(bf)
    result_part = jnp.dot(hidden, gd, preferred_element_type=f).astype(bf).reshape(4, 128, 2048)
    cot = cots.reshape(512, 2048)
    dd = jnp.einsum("tf,td->fd", hidden, cot, preferred_element_type=f).astype(bf)
    grad_hidden = jnp.einsum("td,fd->tf", cot, gd, preferred_element_type=f).astype(bf).astype(f)
    grad_gate = (grad_hidden * upward * sigmoid * (1.0 + gate * (1.0 - sigmoid))).astype(bf)
    grad_up = (grad_hidden * gate * sigmoid).astype(bf)
    dg = jnp.einsum("td,tf->df", entry_two, grad_gate, preferred_element_type=f).astype(bf)
    du = jnp.einsum("td,tf->df", entry_two, grad_up, preferred_element_type=f).astype(bf)
    ge2 = jnp.einsum("tf,df->td", grad_gate, gg, preferred_element_type=f)
    ge2 = ge2 + jnp.einsum("tf,df->td", grad_up, gu, preferred_element_type=f)
    act, gmid, gmls, sums, og, ou, od = back_step(
        ge2.astype(bf).reshape(4, 128, 2048), result_part, mid, cotangent, gains_two,
        dg.reshape(4, 2, 4, 64, 1408), du.reshape(4, 2, 4, 64, 1408), dd.reshape(4, 2, 176, 2048))

    gml = gmls.reshape(512, 2048)
    do = jnp.einsum("td,te->de", mixed, gml, preferred_element_type=f).astype(bf)
    grad_mixed = jnp.einsum("te,de->td", gml, go, preferred_element_type=f).astype(bf).reshape(4, 128, HEADS, HEAD_DIM)
    grad_values = jnp.einsum("shlm,slhd->smhd", probs.astype(bf), grad_mixed, preferred_element_type=f)
    grad_probs = jnp.einsum("slhd,smhd->shlm", grad_mixed, values, preferred_element_type=f)
    grad_scores = (probs * (grad_probs - jnp.sum(probs * grad_probs, axis=-1, keepdims=True))).astype(bf)
    grad_queries = jnp.einsum("shlm,smhd->slhd", grad_scores, keys, preferred_element_type=f) * scale
    grad_keys = jnp.einsum("shlm,slhd->smhd", grad_scores, queries, preferred_element_type=f) * scale
    grad_queries = rotate(grad_queries, cosine, -sine)
    grad_keys = rotate(grad_keys, cosine, -sine)
    grad_projected = jnp.stack([grad_queries, grad_keys, grad_values], axis=2).reshape(512, 1536).astype(bf)
    bias_grad = jnp.sum(grad_projected.astype(f), axis=0).reshape(3, 8, 1, 64)
    here = (lax.broadcasted_iota(jnp.int32, (3, 8, 4, 64), 2) == y).astype(f)
    bias_grad = (bias_grad * here).reshape(32, 3, 64).transpose(1, 0, 2).reshape(3, 2048)
    dq = jnp.einsum("td,te->de", entry_one, grad_projected, preferred_element_type=f).astype(bf)
    ge1 = jnp.einsum("te,de->td", grad_projected, gq, preferred_element_type=f).astype(bf).reshape(4, 128, 2048)
    zero = jnp.zeros((2, 2048), f)
    rows = jnp.concatenate([zero, sums[0:2], bias_grad, zero[:1]])
    gains_one = jnp.concatenate([gs[0:2], jnp.zeros((6, 2048), f)])
    ing, oq, os, oo = last_step(ge1, tokens, gmid, gains_one, rows, dq.reshape(4, 2, 4, 64, 1536), do.reshape(4, 2, 64, 2048))

    os = jnp.sum(os[:, :, :8].astype(f), axis=0)
    qkv_grad = oq.reshape(4, 64, 3, 8, 64).transpose(1, 2, 3, 0, 4).reshape(64, 6144).astype(f)
    gate_grad = og.reshape(4, 64, 8, 176).transpose(1, 2, 0, 3).reshape(64, 5632).astype(f)
    up_grad = ou.reshape(4, 64, 8, 176).transpose(1, 2, 0, 3).reshape(64, 5632).astype(f)
    return (act, ing, os[:, 0], os[:, 1], qkv_grad, os[:, 4:7].T.reshape(192), oo.astype(f),
            os[:, 2], os[:, 3], gate_grad, up_grad, od.astype(f))


def solution(mesh):
    fine = Mesh(mesh.devices.reshape(2, 2, 4, 2, 4), AXES)
    whole, rows = P(AXES, None), P(("z", "xl", "y"), None)
    vector = P(("z", "xl", "y"))
    return jax.shard_map(
        local, mesh=fine,
        in_specs=(whole, whole, whole, vector, vector, rows, vector, rows, vector, vector, rows, rows, rows),
        out_specs=(whole, whole, vector, vector, rows, vector, rows, vector, vector, rows, rows, rows),
        check_vma=False,
    )
```

time: 2710 us -> 564 us (0.21)
  waiting for transfers between devices: 2160 us -> 0 us
  Pallas kernels: 0 us -> 385 us
  blocking collectives: 307 us -> 0 us
  matrix products: 182 us -> 78.8 us
  local copies, waits for them, and re-layouts: 12.4 us -> 74.9 us
    reduce_scatter x5 -> x0, waiting for transfers between devices: 1150 us -> none  [the longest x1 277 us: local(): lax.psum_scatter(down_weight_grad.astype(jnp.bfloat16), 'shard', scatter_...]
    all_gather x5 -> x0, waiting for transfers between devices: 1010 us -> none  [the longest x1 271 us: local(): lax.all_gather(up_weight, 'shard', axis=0, tiled=True)]
    pallas_call x0 -> x4, Pallas kernels: none -> 385 us  [the longest x1 124 us: gather(): pl.pallas_call(gather_kernel, out_shape=outs, in_specs=[hbm] * 9, out_spe...]
    unnamed x2 -> x0, blocking collectives: 272 us -> none
    dot_general x20 -> x19, matrix products: 181 us -> 75.4 us  [the longest x1 7.77 us: local(): ge2 = ge2 + jnp.einsum('tf,df->td', grad_up, gu, preferred_element_type=f)]
    psum x1 -> x0, blocking collectives: 34.6 us -> none  [local(): lax.psum(gain_one_sum.astype(jnp.bfloat16), 'replica').astype(jnp.float32)]
    convert_element_type x1 -> x10, local copies, waits for them, and re-layouts: 2.04 us -> 30 us  [the longest x3 10.5 us: local(): oq.reshape(4, 64, 3, 8, 64).transpose(1, 2, 3, 0, 4).reshape(64, 6144)]
  transfers between devices with their start and end apart: 11 -> 0, of which waited for: 10 -> 0; matrix products, arithmetic and copies ran while one was open for 6% -> 0% of each run, Pallas kernels for 0% -> 0%
where the time goes in v1:
time: 564 us; the launch traced here: 555 us
  Pallas kernels  385 us (68%)
  matrix products  78.8 us (14%)
  local copies, waits for them, and re-layouts  74.9 us (13%)
  other arithmetic  14.7 us (3%)
    pallas_call x1, Pallas kernels, gather(): pl.pallas_call(gather_kernel, out_shape=outs, in_specs=[hbm] * 9, out_spe...  124 us
    pallas_call x1, Pallas kernels, back_step(): pl.pallas_call(back_kernel, out_shape=(S((128, 2048), bf), S((128, 2048),...  113 us
    pallas_call x1, Pallas kernels, last_step(): pl.pallas_call(last_kernel, out_shape=(S((128, 2048), bf), S((4, 64, 1536...  95.6 us
    pallas_call x1, Pallas kernels, middle_step(): pl.pallas_call(middle_kernel, out_shape=(S((128, 2048), jnp.float32), S((...  52.5 us

profile of v1, /device:TPU:1, one launch (start us, length us, event | category | flops | bytes accessed | tf_op | source)
XLA Modules:
  0.0 555.2 jit_solution(9020650151049128381)
XLA Ops:
  1.9 2.5 reshape.269
  16.4 123.7 %gather.1 = (bf16[4,128,2048]{2,1,0:T(8,128)(2,1)}, bf16[4,128,2048]{2,1,0:T(8,128)(2,1)}, f32[4,8,128]{2,1,0:T(8,128)}, bf16[4,2,4,64,1536]{4,3,2,1,0:T(8,128)(...) custom-call(bf16[128,2048]{1,0:T(8,128)(2,1)} %tok.5, ...), custom_call_target="tpu_custom_call" | custom-call | tf_op jit(solution)/shard_map/gather/pallas_call | solution.py:150
  144.1 2.3 fusion.6
  146.7 6.4 %convolution_add_fusion = f32[512,1536]{1,0:T(8,128)S(1)} fusion(bf16[512,2048]{1,0:T(8,128)(2,1)} %bitcast.148, bf16[2048,1536]{1,0:T(8,128)(2,1)} %bitcast.169, f32[1536]{0:T(1024)S(1)} %add.66), kind=kOutput, calls=%fused_computation.16 | convolution fusion | flops 3222011904 | bytes 11540480 | tf_op jit(solution)/shard_map/dot_general | solution.py:520
  153.1 3.5 reshape.306
  161.2 3.8 fusion.46
  172.8 2.5 fusion.48
  179.3 52.5 %middle_step.1 = (f32[128,2048]{1,0:T(8,128)S(1)}, bf16[4,128,2048]{2,1,0:T(8,128)(2,1)S(1)}) custom-call(bf16[4,128,2048]{2,1,0:T(8,128)(2,1)S(1)} %bitcast.129, bf16[128,2048]{1,0:T(8,128)(2,1)S(1)} %copy-done, f32[8,2048]{1,0:T(8,128)S(1)} %concatenate.31.gains), custom_call_target="tpu_custom_call" | custom-call | tf_op jit(solution)/shard_map/middle_step/pallas_call | solution.py:319
  231.9 3.4 fusion.49
  235.4 3.5 convolution_convert_fusion.7
  238.9 5.2 multiply_convert_fusion
  245.2 5.0 fusion.50
  250.2 7.8 %add_convert_fusion = bf16[512,2048]{1,0:T(8,128)(2,1)} fusion(f32[512,2048]{1,0:T(8,128)} %fusion.50, bf16[2048,1408]{1,0:T(8,128)(2,1)S(1)} %bitcast.180, f32[512,1408]{1,0:T(8,128)} %copy-done.45, bf16[512,1408]{1,0:T(8,128)(2,1)} %copy-done.47), kind=kOutput, calls=%fused_computation.13 | convolution fusion | flops 2959933440 | bytes 16384000 | tf_op jit(solution)/shard_map/tf,df->td/dot_general | solution.py:549
  257.9 4.7 convolution_convert_fusion.8
  262.6 5.5 convolution_convert_fusion.3
  268.2 5.5 convolution_convert_fusion.2
  273.7 5.0 convolution_convert_fusion.1
  278.8 113.1 %back_step.1 = (bf16[128,2048]{1,0:T(8,128)(2,1)}, f32[128,2048]{1,0:T(8,128)}, bf16[4,128,2048]{2,1,0:T(8,128)(2,1)}, f32[8,2048]{1,0:T(8,128)}, bf16[4,64,1408...) custom-call(bf16[4,128,2048]{2,1,0:T(8,128)(2,1)} %bitcast.152, ...), custom_call_target="tpu_custom_call" | custom-call | tf_op jit(solution)/shard_map/back_step/pallas_call | solution.py:389
  391.8 3.7 convolution_convert_fusion.9
  406.4 4.8 convolution_convert_fusion.5
  413.9 7.0 %convolution_convert_fusion = bf16[2048,1536]{1,0:T(8,128)(2,1)} fusion(bf16[512,2048]{1,0:T(8,128)(2,1)S(1)} %bitcast.149, bf16[192,8,4,128]{3,2,1,0:T(4,128)(2,1)} %bitcast.155), kind=kOutput, calls=%fused_computation.1 | convolution fusion | flops 3224371200 | bytes 9961472 | tf_op jit(solution)/shard_map/td,te->de/dot_general | solution.py:568
  420.8 2.6 convolution_convert_fusion.4
  423.4 95.6 %last_step.1 = (bf16[128,2048]{1,0:T(8,128)(2,1)}, bf16[4,64,1536]{2,1,0:T(8,128)(2,1)}, bf16[4,64,128]{2,1,0:T(8,128)(2,1)}, bf16[64,2048]{1,0:T(8,128)(2,1)}) custom-call(bf16[4,128,2048]{2,1,0:T(8,128)(2,1)} %bitcast.150, bf16[128,2048]{1,0:T(8,128)(2,1)} %tok.5, f32[128,2048]{1,0:T(8,128)} %get-tuple-element.47.gmid, ...), custom_call_target="tpu_custom_call" | custom-call | tf_op jit(solution)/shard_map/last_step/pallas_call | solution.py:453
  520.6 3.4 reshape.303
  523.9 3.9 copy.124
  527.9 3.2 reshape.300
  532.7 3.5 reshape.304
  536.2 2.9 copy.126
  539.1 3.5 reshape.301
  542.7 2.7 reshape.305
  545.4 2.9 copy.127
  548.4 3.5 reshape.302
  (206 shorter events, 54.2 us)
Async XLA Ops:
  4.7 3.2 copy-start.8
  140.0 3.4 copy-start.3
  141.4 5.0 copy-start.28
  171.6 3.8 copy-start.22
  171.6 3.8 copy-start.24
  175.4 56.4 %slice-start.6 = ((s8[5767168]{0:T(1024)(128)(4,1)}), s8[4194304]{0:T(1024)(128)(4,1)S(1)}, s32[]{:S(2)}) async-start(s8[5767168]{0:T(1024)(128)(4,1)} %bitcast.181), calls=%async_computation.6 | async-start | bytes 8388608
  177.1 54.7 %slice-start.7 = ((s8[5767168]{0:T(1024)(128)(4,1)}), s8[1572864]{0:T(1024)(128)(4,1)S(1)}, s32[]{:S(2)}) async-start(s8[5767168]{0:T(1024)(128)(4,1)} %bitcast.181), calls=%async_computation.7 | async-start | bytes 3145728
  179.3 56.0 %copy-start.2 = (f32[8,2048]{1,0:T(8,128)}, f32[8,2048]{1,0:T(8,128)S(1)}, u32[]{:S(2)}) copy-start(f32[8,2048]{1,0:T(8,128)S(1)} %concatenate.31.gains) | copy-start | bytes 196612
  179.3 56.0 %slice-start.2 = ((s8[5767168]{0:T(1024)(128)(4,1)}), s8[4194304]{0:T(1024)(128)(4,1)S(1)}, s32[]{:S(2)}) async-start(s8[5767168]{0:T(1024)(128)(4,1)} %bitcast.173), calls=%async_computation.2 | async-start | bytes 8388608
  179.3 59.5 %slice-start.4 = ((s8[5767168]{0:T(1024)(128)(4,1)}), s8[4194304]{0:T(1024)(128)(4,1)S(1)}, s32[]{:S(2)}) async-start(s8[5767168]{0:T(1024)(128)(4,1)} %bitcast.177), calls=%async_computation.4 | async-start | bytes 8388608
  231.8 3.5 copy-start.1
  231.8 3.5 slice-start.3
  231.9 3.5 copy-start.38
  231.9 7.0 %slice-start.5 = ((s8[5767168]{0:T(1024)(128)(4,1)}), s8[1572864]{0:T(1024)(128)(4,1)S(1)}, s32[]{:S(2)}) async-start(s8[5767168]{0:T(1024)(128)(4,1)} %bitcast.177), calls=%async_computation.5 | async-start | bytes 3145728
  235.3 3.5 copy-start.45
  238.8 5.2 copy-start.47
  250.2 7.8 %copy-start.42 = (bf16[512,1408]{1,0:T(8,128)(2,1)S(1)}, bf16[512,1408]{1,0:T(8,128)(2,1)}, u32[]{:S(2)}) copy-start(bf16[512,1408]{1,0:T(8,128)(2,1)} %get-tuple-element.64) | copy-start | bytes 4325380
  257.9 4.7 copy-start.44
  262.6 5.5 copy-start.46
  262.6 5.5 copy-start.48
  268.2 5.5 copy-start.39
  278.7 113.1 %copy-start.37 = (bf16[4,2,64,2048]{3,2,1,0:T(8,128)(2,1)S(1)}, bf16[4,2,64,2048]{3,2,1,0:T(8,128)(2,1)}, u32[]{:S(2)}) copy-start(bf16[4,2,64,2048]{3,2,1,0:T(8,128)(2,1)} %get-tuple-element.40) | copy-start | bytes 6291460
  406.3 4.8 copy-start.5
  406.3 4.8 copy-start.20
  406.3 4.8 copy-start.31
  406.4 7.5 %copy-start.4 = (bf16[4,128,2048]{2,1,0:T(8,128)(2,1)S(1)}, bf16[4,128,2048]{2,1,0:T(8,128)(2,1)}, u32[]{:S(2)}) copy-start(bf16[4,128,2048]{2,1,0:T(8,128)(2,1)} %fusion.6) | copy-start | bytes 6291460
  413.9 7.0 %copy-start.17 = (bf16[4,128,8,64]{1,0,3,2:T(4,128)(2,1)S(1)}, bf16[4,128,8,64]{1,0,3,2:T(4,128)(2,1)}, u32[]{:S(2)}) copy-start(bf16[4,128,8,64]{1,0,3,2:T(4,128)(2,1)} %copy-done.16) | copy-start | bytes 1572868
  413.9 7.0 %copy-start.40 = (bf16[4,128,2048]{2,1,0:T(8,128)(2,1)S(1)}, bf16[4,128,2048]{2,1,0:T(8,128)(2,1)}, u32[]{:S(2)}) copy-start(bf16[4,128,2048]{2,1,0:T(8,128)(2,1)} %get-tuple-element.46) | copy-start | bytes 6291460
  527.9 4.0 copy-start.21
  539.1 3.5 copy-start.11
  548.3 3.5 copy-start.10
  548.4 4.8 copy-start.15
  (25 other events, 46.8 us)
